TPU v7x, 512 devices: a whole 4x8x8 slice. The times are simulated.
512 devices in a mesh: row: 32 (over x, y), span: 16 (over z, core).
Axes of the slice: x: 4, y: 8, z: 8, core: 2. Of those that a mesh axis runs over, the one named last changes fastest.
Arguments:
- velocity: float32 [3, 16, 512, 4096], P(None, 'span', 'row'), may hold values from -6 to 6
- row_counts: int32 [32], replicated, may hold values from 1 to 16, as said below
- y_metric: float32 [257], replicated, may hold values from 0.5 to 2
- y_curvature: float32 [257], replicated, may hold values from -3 to 3
Outputs:
- rhs: float32 [3, 16, 512, 4096], P(None, 'span', 'row')
Inputs may be any that keep to these rules, and one draw needn't show every extreme that they name: Index r of row holds row_counts[r] grid rows in its first row_counts[r] slots, following those of index r - 1; the counts sum to 257.
All inputs are finite; a program needn't handle non-finite values.
Results may differ from a plain program's by a relative error of at most 0.000059.
Values sent between devices are 32-bit elements; how exact they have to be, the bound alone decides.
A program may use at most 64 MiB of HBM per device.

v0:
```python
import functools
import math

import jax
import jax.numpy as jnp
import ml_dtypes
import numpy as np
from jax import lax
from jax.experimental import pallas as pl
from jax.experimental.pallas import tpu as pltpu
from jax.sharding import PartitionSpec as P

MESH = pl.DeviceIdType.MESH
viscosity = 0.2
LANES = 128
STATES = 8


def scheme(alpha, first):
    root = math.sqrt(1.0 - 4.0 * alpha * alpha)
    decay = (1.0 - root) / (2.0 * alpha)

    def res(s):
        return (-decay) ** abs(s) / root

    def tap(s):
        if first:
            return 0.5 * 14.0 / 9.0 * (res(s - 1) - res(s + 1)) + 0.25 / 9.0 * (res(s - 2) - res(s + 2))
        return (
            12.0 / 11.0 * (res(s - 1) - 2.0 * res(s) + res(s + 1))
            + 0.25 * 3.0 / 11.0 * (res(s - 2) - 2.0 * res(s) + res(s + 2))
        )

    amp = tap(2) / decay**2
    return dict(tap=tap, log=math.log(decay), amp=amp, near=tap(1) + amp * decay, centre=tap(0))


FIRST = scheme(1.0 / 3.0, True)
SECOND = scheme(2.0 / 11.0, False)


def split_table(table):
    high = table.astype(ml_dtypes.bfloat16)
    return jnp.asarray(high), jnp.asarray((table - high.astype(np.float64)).astype(ml_dtypes.bfloat16))


def line_table():
    table = np.zeros((2 * LANES, 2 * LANES))
    for p in range(2 * LANES):
        for q in range(LANES):
            shift = p - LANES // 2 - q
            table[p, q] = FIRST["tap"](shift)
            table[p, LANES + q] = viscosity * SECOND["tap"](shift)
    return table


def plane_table(count):
    table = np.zeros((2, count, 8, count, 8))
    for m in range(count):
        for n in range(count):
            for turn in range(-40, 41):
                shift = n - m + turn * count
                for row in range(8):
                    table[0, m, row, n, row] += FIRST["tap"](shift)
                    table[1, m, row, n, row] += viscosity * SECOND["tap"](shift)
    return table.reshape(16 * count, 8 * count)


def split(values):
    high = values.astype(jnp.bfloat16)
    return high, (values - high.astype(jnp.float32)).astype(jnp.bfloat16)


def product(left, right):
    dot = functools.partial(jnp.dot, preferred_element_type=jnp.float32)
    return dot(left[0], right[0]) + (dot(left[0], right[1]) + dot(left[1], right[0]))


def power(log, steps):
    size = jnp.exp(steps.astype(jnp.float32) * log)
    return jnp.where(steps % 2 == 0, size, -size)


def iota(shape, axis):
    return lax.broadcasted_iota(jnp.int32, shape, axis)


def partner(index, me, count):
    half = count // 2
    step = jnp.where(index % 2 == 1, half - (index + 1) // 2, half + index // 2)
    return (me + step) % count


def kernel(
    ranks, planes, live_total, length,
    v, counts, metric, curvature, line_high, line_low, plane_high, plane_low,
    out,
    pad_high, pad_low, z_in, z_out, z_back, s_out, s_in, s_mid, s_back, s_weight, y_weight,
    z_send, z_recv, zb_send, zb_recv, s_send, s_recv, sb_send, sb_recv,
):
    my_row, my_plane = lax.axis_index("row"), lax.axis_index("span")
    z_cols, s_cols = length // planes, length // ranks
    pieces = [(half, part) for half in range(2) for part in range(z_cols // LANES)]

    def lanes(start, size=LANES):
        return pl.ds(pl.multiple_of(start, LANES), size)

    def forth(piece, source, target):
        half, part = pieces[piece]
        return pltpu.make_async_remote_copy(
            src_ref=v.at[:, half, :, lanes(target * z_cols + part * LANES)],
            dst_ref=z_in.at[piece, source],
            send_sem=z_send.at[piece, target],
            recv_sem=z_recv.at[piece, source],
            device_id={"span": target},
            device_id_type=MESH,
        )

    def back(piece, source, target):
        half, part = pieces[piece]
        return pltpu.make_async_remote_copy(
            src_ref=z_out.at[piece, target],
            dst_ref=z_back.at[:, half, :, lanes(source * z_cols + part * LANES)],
            send_sem=zb_send.at[piece, target],
            recv_sem=zb_recv.at[piece, source],
            device_id={"span": target},
            device_id_type=MESH,
        )

    def state_forth(source, target):
        return pltpu.make_async_remote_copy(
            src_ref=s_out.at[:, :, lanes(target * s_cols, s_cols)],
            dst_ref=s_in.at[source],
            send_sem=s_send.at[target],
            recv_sem=s_recv.at[source],
            device_id={"row": target},
            device_id_type=MESH,
        )

    def state_back(source, target):
        return pltpu.make_async_remote_copy(
            src_ref=s_mid.at[target],
            dst_ref=s_back.at[:, :, lanes(source * s_cols, s_cols)],
            send_sem=sb_send.at[target],
            recv_sem=sb_recv.at[source],
            device_id={"row": target},
            device_id_type=MESH,
        )

    def over_planes(act):
        pl.loop(0, planes - 1)(lambda index: act(partner(index, my_plane, planes)))

    def over_ranks(act):
        pl.loop(0, ranks - 1)(lambda index: act(partner(index, my_row, ranks)))

    barrier = pltpu.get_barrier_semaphore()
    over_planes(lambda p: pl.semaphore_signal(barrier, 1, device_id={"span": p}, device_id_type=MESH))
    over_ranks(lambda p: pl.semaphore_signal(barrier, 1, device_id={"row": p}, device_id_type=MESH))

    count = counts[my_row]
    start = jnp.int32(0)
    for rank in range(ranks):
        start = start + jnp.where(rank < my_row, counts[rank], 0)

    kind = iota((STATES, LANES), 0)
    decay_log = jnp.where(kind % 2 == 0, FIRST["log"], SECOND["log"])
    for k in range(16):
        steps = jnp.where(kind < 2, jnp.maximum(count - 1 - k, 0), k)
        weight = jnp.where(kind < 4, power(decay_log, steps), 0.0)
        weight = jnp.where((kind == 4) & (k == 0), 1.0, weight)
        weight = jnp.where((kind == 5) & (count - 1 == k), 1.0, weight)
        s_weight[k] = jnp.where(k < count, weight, 0.0)

    pl.semaphore_wait(barrier, planes + ranks - 2)

    for piece in range(len(pieces)):
        over_planes(lambda p, piece=piece: forth(piece, my_plane, p).start())

    @pl.loop(0, length // LANES)
    def _(tile):
        at = lanes(tile * LANES)
        for c in range(3):
            total = jnp.zeros((STATES, LANES), jnp.float32)
            for k in range(16):
                total = total + s_weight[k] * v[c, k // 8, pl.ds(k % 8, 1), at]
            s_out[c, :, at] = total

    over_ranks(lambda p: state_forth(my_row, p).start())
    s_in[my_row] = s_out[:, :, lanes(my_row * s_cols, s_cols)]
    for piece, (half, part) in enumerate(pieces):
        z_in[piece, my_plane] = v[:, half, :, lanes(my_plane * z_cols + part * LANES)]

    for c in range(3):
        turned = pltpu.roll(v[c].reshape(16, length), LANES // 2, 1)
        high, low = split(turned)
        rows = pl.ds(16 * c, 16)
        pad_high[rows, pl.ds(0, length)] = high
        pad_low[rows, pl.ds(0, length)] = low
        pad_high[rows, pl.ds(length, LANES)] = high[:, :LANES]
        pad_low[rows, pl.ds(length, LANES)] = low[:, :LANES]

    group = 4

    def along_x(step):
        def windows(ref):
            return jnp.concatenate(
                [ref[:, lanes((step * group + i) * LANES, 2 * LANES)] for i in range(group)], axis=0
            )

        both = product((windows(pad_high), windows(pad_low)), (line_high[...], line_low[...]))
        for i in range(group):
            at = lanes((step * group + i) * LANES)
            wind = v[0, :, :, at].reshape(16, LANES)
            for c in range(3):
                rows = slice(48 * i + 16 * c, 48 * i + 16 * c + 16)
                part = both[rows, LANES:] - wind * both[rows, :LANES]
                out[c, :, :, at] = part.reshape(2, 8, LANES)

    steps_x = length // (LANES * group)
    pl.loop(0, steps_x // 2)(along_x)

    def along_z(piece):
        over_planes(lambda p: forth(piece, p, my_plane).wait_recv())
        held = [z_in[piece, :, c].reshape(8 * planes, LANES) for c in range(3)]
        both = product((plane_high[...], plane_low[...]), split(jnp.concatenate(held, axis=1)))
        for c in range(3):
            at = slice(c * LANES, (c + 1) * LANES)
            part = both[8 * planes :, at] - held[2] * both[: 8 * planes, at]
            z_out[piece, :, c] = part.reshape(planes, 8, LANES)
        over_planes(lambda p: back(piece, my_plane, p).start())
        half, part = pieces[piece]
        z_back[:, half, :, lanes(my_plane * z_cols + part * LANES)] = z_out[piece, my_plane]

    def over_y():
        size = ranks * STATES
        row_rank, row_kind = iota((size, size), 0) // STATES, iota((size, size), 0) % STATES
        col_rank, col_kind = iota((size, size), 1) // STATES, iota((size, size), 1) % STATES
        row_start = row_count = col_start = col_count = jnp.zeros((size, size), jnp.int32)
        for rank in range(ranks):
            held = counts[rank]
            row_start = row_start + jnp.where(rank < row_rank, held, 0)
            col_start = col_start + jnp.where(rank < col_rank, held, 0)
            row_count = jnp.where(rank == row_rank, held, row_count)
            col_count = jnp.where(rank == col_rank, held, col_count)
        ahead = row_start - col_start - col_count
        ahead = jnp.where(ahead < 0, ahead + live_total, ahead)
        behind = col_start - row_start - row_count
        behind = jnp.where(behind < 0, behind + live_total, behind)
        log = jnp.where(row_kind % 2 == 0, FIRST["log"], SECOND["log"])
        same = power(log, jnp.where(row_kind < 2, ahead, behind))
        matrix = jnp.where((row_kind == col_kind) & (row_kind < 4), same, 0.0)
        matrix = jnp.where((row_kind == 4) & (col_kind == 5) & (ahead == 0), 1.0, matrix)
        matrix = jnp.where((row_kind == 5) & (col_kind == 4) & (behind == 0), 1.0, matrix)
        matrix = split(matrix)
        over_ranks(lambda p: state_forth(p, my_row).wait_recv())
        held = [s_in[:, c].reshape(size, s_cols) for c in range(3)]
        both = product(matrix, split(jnp.concatenate(held, axis=1)))
        for c in range(3):
            s_mid[:, c] = both[:, c * s_cols : (c + 1) * s_cols].reshape(ranks, STATES, s_cols)
        over_ranks(lambda p: state_back(my_row, p).start())
        s_back[:, :, lanes(my_row * s_cols, s_cols)] = s_mid[my_row]

    along_z(0)
    pl.loop(steps_x // 2, steps_x)(along_x)
    along_z(1)
    over_y()
    for piece in range(2, len(pieces)):
        along_z(piece)

    for half in range(2):
        slot = iota((8, LANES), 0) + 8 * half
        stretch = jnp.zeros((8, LANES), jnp.float32)
        bend = jnp.zeros((8, LANES), jnp.float32)
        for k in range(8 * half, 8 * half + 8):
            grid_row = jnp.minimum(start + k, live_total - 1)
            stretch = jnp.where(slot == k, metric[grid_row], stretch)
            bend = jnp.where(slot == k, curvature[grid_row], bend)
        live = slot < count
        tail = jnp.maximum(count - slot, 0)
        for term in range(16 + 6):
            if term < 16:
                away = jnp.abs(term - slot)
                one = FIRST["amp"] * power(FIRST["log"], away) + jnp.where(away == 1, FIRST["near"], 0.0)
                one = jnp.where(away == 0, 0.0, jnp.where(term > slot, one, -one))
                two = SECOND["amp"] * power(SECOND["log"], away) + jnp.where(away == 1, SECOND["near"], 0.0)
                two = jnp.where(away == 0, SECOND["centre"], two)
                used = live & (term < count)
            else:
                one = two = jnp.zeros((8, LANES), jnp.float32)
                used = live
                if term == 16:
                    one = -FIRST["amp"] * power(FIRST["log"], slot + 1)
                if term == 17:
                    two = SECOND["amp"] * power(SECOND["log"], slot + 1)
                if term == 18:
                    one = FIRST["amp"] * power(FIRST["log"], tail)
                if term == 19:
                    two = SECOND["amp"] * power(SECOND["log"], tail)
                if term == 20:
                    one = jnp.where(slot == 0, -FIRST["near"], 0.0)
                    two = jnp.where(slot == 0, SECOND["near"], 0.0)
                if term == 21:
                    one = jnp.where(tail == 1, FIRST["near"], 0.0)
                    two = jnp.where(tail == 1, SECOND["near"], 0.0)
            y_weight[term, half, 0] = jnp.where(used, stretch * one, 0.0)
            y_weight[term, half, 1] = jnp.where(
                used, viscosity * (stretch * stretch * two + bend * one), 0.0
            )

    over_ranks(lambda p: state_back(p, my_row).wait_recv())

    @pl.loop(0, length // LANES)
    def _(tile):
        at = lanes(tile * LANES)
        sums = [[[jnp.zeros((8, LANES), jnp.float32)] * 2 for _ in range(2)] for _ in range(3)]
        for term in range(16 + 6):
            for c in range(3):
                if term < 16:
                    line = v[c, term // 8, pl.ds(term % 8, 1), at]
                else:
                    line = s_back[c, pl.ds(term - 16, 1), at]
                for half in range(2):
                    sums[c][half] = [sums[c][half][i] + y_weight[term, half, i] * line for i in range(2)]
        for half in range(2):
            wind = v[1, half, :, at]
            for c in range(3):
                out[c, half, :, at] += sums[c][half][1] - wind * sums[c][half][0]

    per_half = len(pieces) // 2
    for half in range(2):
        for piece in range(half * per_half, (half + 1) * per_half):
            over_planes(lambda p, piece=piece: back(piece, p, my_plane).wait_recv())
        live = iota((8, LANES), 0) + 8 * half < count

        @pl.loop(0, length // LANES)
        def _(tile, half=half, live=live):
            at = lanes(tile * LANES)
            for c in range(3):
                out[c, half, :, at] = jnp.where(live, out[c, half, :, at] + z_back[c, half, :, at], 0.0)

    for piece in range(len(pieces)):
        over_planes(lambda p, piece=piece: forth(piece, my_plane, p).wait_send())
        over_planes(lambda p, piece=piece: back(piece, my_plane, p).wait_send())
    over_ranks(lambda p: state_forth(my_row, p).wait_send())
    over_ranks(lambda p: state_back(my_row, p).wait_send())


def local(ranks, planes, velocity, row_counts, y_metric, y_curvature):
    length = velocity.shape[3]
    live_total = y_metric.shape[0]
    z_cols, s_cols = length // planes, length // ranks
    pieces = 2 * z_cols // LANES
    vmem = pl.BlockSpec(memory_space=pltpu.VMEM)
    smem = pl.BlockSpec(memory_space=pltpu.SMEM)
    whole = (3, 2, 8, length)
    dma = pltpu.SemaphoreType.DMA
    f32 = jnp.float32
    result = pl.pallas_call(
        functools.partial(kernel, ranks, planes, live_total, length),
        out_shape=jax.ShapeDtypeStruct(whole, f32),
        in_specs=[vmem, smem, smem, smem, vmem, vmem, vmem, vmem],
        out_specs=vmem,
        scratch_shapes=[
            pltpu.VMEM((48, length + LANES), jnp.bfloat16),
            pltpu.VMEM((48, length + LANES), jnp.bfloat16),
            pltpu.VMEM((pieces, planes, 3, 8, LANES), f32),
            pltpu.VMEM((pieces, planes, 3, 8, LANES), f32),
            pltpu.VMEM(whole, f32),
            pltpu.VMEM((3, STATES, length), f32),
            pltpu.VMEM((ranks, 3, STATES, s_cols), f32),
            pltpu.VMEM((ranks, 3, STATES, s_cols), f32),
            pltpu.VMEM((3, STATES, length), f32),
            pltpu.VMEM((16, STATES, LANES), f32),
            pltpu.VMEM((22, 2, 2, 8, LANES), f32),
            dma((pieces, planes)),
            dma((pieces, planes)),
            dma((pieces, planes)),
            dma((pieces, planes)),
            dma((ranks,)),
            dma((ranks,)),
            dma((ranks,)),
            dma((ranks,)),
        ],
        compiler_params=pltpu.CompilerParams(
            collective_id=0, has_side_effects=True, vmem_limit_bytes=32 * 1024 * 1024
        ),
        cost_estimate=pl.CostEstimate(flops=10**9, bytes_accessed=2 * 10**6, transcendentals=10**5),
    )(
        velocity.reshape(whole), row_counts, y_metric, y_curvature,
        *split_table(line_table()), *split_table(plane_table(planes)),
    )
    return result.reshape(velocity.shape)


def solution(mesh):
    return jax.shard_map(
        functools.partial(local, mesh.shape["row"], mesh.shape["span"]),
        mesh=mesh,
        in_specs=(P(None, "span", "row", None), P(), P(), P()),
        out_specs=P(None, "span", "row", None),
        check_vma=False,
    )
```

profile of v0, /device:TPU:1, one launch (start us, length us, event | category | flops | bytes accessed | tf_op | source)
XLA Modules:
  0.0 69.8 jit_solution(6754791390741821296)
XLA Ops:
  0.0 0.0 copy-start.3
  0.0 0.7 copy-done.3
  0.7 0.0 copy-start
  0.7 1.1 %copy-done = f32[3,1,16,4096]{3,2,1,0:T(8,128)S(1)} copy-done((f32[3,1,16,4096]{3,2,1,0:T(8,128)S(1)}, f32[3,1,16,4096]{3,2,1,0:T(8,128)}, u32[]{:S(2)}) %copy-start) | copy-done | bytes 786456
  1.8 0.0 copy-start.1
  1.8 0.7 copy-done.1
  2.5 0.0 copy-start.2
  2.5 0.7 copy-done.2
  3.2 0.0 copy-start.4
  3.2 0.9 %copy-done.4 = bf16[256,256]{1,0:T(8,128)(2,1)S(1)} copy-done((bf16[256,256]{1,0:T(8,128)(2,1)S(1)}, bf16[256,256]{1,0:T(8,128)(2,1)}, u32[]{:S(2)}) %copy-start.4) | copy-done | bytes 131096
  4.1 0.0 copy-start.5
  4.1 0.9 %copy-done.5 = bf16[256,256]{1,0:T(8,128)(2,1)S(1)} copy-done((bf16[256,256]{1,0:T(8,128)(2,1)S(1)}, bf16[256,256]{1,0:T(8,128)(2,1)}, u32[]{:S(2)}) %copy-start.5) | copy-done | bytes 131096
  5.0 0.0 copy-start.6
  5.0 0.8 %copy-done.6 = bf16[256,128]{1,0:T(8,128)(2,1)S(1)} copy-done((bf16[256,128]{1,0:T(8,128)(2,1)S(1)}, bf16[256,128]{1,0:T(8,128)(2,1)}, u32[]{:S(2)}) %copy-start.6) | copy-done | bytes 65560
  5.8 0.0 copy-start.7
  5.8 0.8 %copy-done.7 = bf16[256,128]{1,0:T(8,128)(2,1)S(1)} copy-done((bf16[256,128]{1,0:T(8,128)(2,1)S(1)}, bf16[256,128]{1,0:T(8,128)(2,1)}, u32[]{:S(2)}) %copy-start.7) | copy-done | bytes 65560
  6.6 62.3 %shard_map.82 = f32[3,2,8,4096]{3,2,1,0:T(8,128)S(1)} custom-call(f32[3,2,8,4096]{3,2,1,0:T(8,128)S(1)} %bitcast.5, s32[32]{0:T(128)S(1)} %copy-done.3, f32[257]{0:T(512)S(1)} %copy-done.1, f32[257]{0:T(512)S(1)} %copy-done.2, bf16[256,256]{1,0:T(8,128)(2,1)S(1)} %copy-done.5, bf16[256,256]{1,0:T(8,128)(2,1)S(1)} %copy-done.4, ...), custom_call_target="tpu_custom_call" | custom-call | flops 1000000000 | bytes 2000000 | tf_op jit(solution)/shard_map/pallas_call | solution.py:358
  68.9 0.9 %copy.11 = f32[3,1,16,4096]{3,2,1,0:T(8,128)} copy(f32[3,1,16,4096]{3,2,1,0:T(8,128)S(1)} %bitcast.4) | data formatting | bytes 1572864
Async XLA Ops:
  0.0 0.7 copy-start.3
  0.7 1.1 %copy-start = (f32[3,1,16,4096]{3,2,1,0:T(8,128)S(1)}, f32[3,1,16,4096]{3,2,1,0:T(8,128)}, u32[]{:S(2)}) copy-start(f32[3,1,16,4096]{3,2,1,0:T(8,128)} %param.8) | copy-start | bytes 2359300
  1.8 0.7 copy-start.1
  2.5 0.7 copy-start.2
  3.2 0.9 %copy-start.4 = (bf16[256,256]{1,0:T(8,128)(2,1)S(1)}, bf16[256,256]{1,0:T(8,128)(2,1)}, u32[]{:S(2)}) copy-start(bf16[256,256]{1,0:T(8,128)(2,1)} %constant.9.clone.line_low) | copy-start | bytes 393220
  4.1 0.9 %copy-start.5 = (bf16[256,256]{1,0:T(8,128)(2,1)S(1)}, bf16[256,256]{1,0:T(8,128)(2,1)}, u32[]{:S(2)}) copy-start(bf16[256,256]{1,0:T(8,128)(2,1)} %constant.8.clone.line_high) | copy-start | bytes 393220
  5.0 0.8 %copy-start.6 = (bf16[256,128]{1,0:T(8,128)(2,1)S(1)}, bf16[256,128]{1,0:T(8,128)(2,1)}, u32[]{:S(2)}) copy-start(bf16[256,128]{1,0:T(8,128)(2,1)} %constant.11.clone.plane_low) | copy-start | bytes 196612
  5.8 0.8 %copy-start.7 = (bf16[256,128]{1,0:T(8,128)(2,1)S(1)}, bf16[256,128]{1,0:T(8,128)(2,1)}, u32[]{:S(2)}) copy-start(bf16[256,128]{1,0:T(8,128)(2,1)} %constant.10.clone.plane_high) | copy-start | bytes 196612
where the time goes:
time: 70.1 us; the launch traced here: 69.8 us
  Pallas kernels  62.3 us (89%)
  local copies, waits for them, and re-layouts  7.52 us (11%)
    pallas_call x1, Pallas kernels, local(): pl.pallas_call(functools.partial(kernel, ranks, planes, live_total, lengt...  62.3 us
    unnamed x17, local copies, waits for them, and re-layouts  7.52 us

commit v1 on v0

--- a/solution.py
+++ b/solution.py
@@ -3,7 +3,6 @@
 
 import jax
 import jax.numpy as jnp
-import ml_dtypes
 import numpy as np
 from jax import lax
 from jax.experimental import pallas as pl
@@ -37,11 +36,6 @@
 
 FIRST = scheme(1.0 / 3.0, True)
 SECOND = scheme(2.0 / 11.0, False)
-
-
-def split_table(table):
-    high = table.astype(ml_dtypes.bfloat16)
-    return jnp.asarray(high), jnp.asarray((table - high.astype(np.float64)).astype(ml_dtypes.bfloat16))
 
 
 def line_table():
@@ -93,36 +87,34 @@
 
 def kernel(
     ranks, planes, live_total, length,
-    v, counts, metric, curvature, line_high, line_low, plane_high, plane_low,
-    out,
+    v_far, counts_far, metric_far, curvature_far, line_far, plane_far,
+    out_far,
+    out, v, counts, metric, curvature, line, plane, line_high, line_low, plane_high, plane_low, matrix,
     pad_high, pad_low, z_in, z_out, z_back, s_out, s_in, s_mid, s_back, s_weight, y_weight,
-    z_send, z_recv, zb_send, zb_recv, s_send, s_recv, sb_send, sb_recv,
+    local_sem, z_send, z_recv, zb_send, zb_recv, s_send, s_recv, sb_send, sb_recv,
 ):
     my_row, my_plane = lax.axis_index("row"), lax.axis_index("span")
     z_cols, s_cols = length // planes, length // ranks
-    pieces = [(half, part) for half in range(2) for part in range(z_cols // LANES)]
 
     def lanes(start, size=LANES):
         return pl.ds(pl.multiple_of(start, LANES), size)
 
-    def forth(piece, source, target):
-        half, part = pieces[piece]
+    def forth(half, source, target):
         return pltpu.make_async_remote_copy(
-            src_ref=v.at[:, half, :, lanes(target * z_cols + part * LANES)],
-            dst_ref=z_in.at[piece, source],
-            send_sem=z_send.at[piece, target],
-            recv_sem=z_recv.at[piece, source],
+            src_ref=v_far.at[:, half, :, lanes(target * z_cols, z_cols)],
+            dst_ref=z_in.at[half, source],
+            send_sem=z_send.at[half, target],
+            recv_sem=z_recv.at[half, source],
             device_id={"span": target},
             device_id_type=MESH,
         )
 
-    def back(piece, source, target):
-        half, part = pieces[piece]
+    def back(half, source, target):
         return pltpu.make_async_remote_copy(
-            src_ref=z_out.at[piece, target],
-            dst_ref=z_back.at[:, half, :, lanes(source * z_cols + part * LANES)],
-            send_sem=zb_send.at[piece, target],
-            recv_sem=zb_recv.at[piece, source],
+            src_ref=z_out.at[half, target],
+            dst_ref=z_back.at[:, half, :, lanes(source * z_cols, z_cols)],
+            send_sem=zb_send.at[half, target],
+            recv_sem=zb_recv.at[half, source],
             device_id={"span": target},
             device_id_type=MESH,
         )
@@ -156,12 +148,14 @@
     barrier = pltpu.get_barrier_semaphore()
     over_planes(lambda p: pl.semaphore_signal(barrier, 1, device_id={"span": p}, device_id_type=MESH))
     over_ranks(lambda p: pl.semaphore_signal(barrier, 1, device_id={"row": p}, device_id_type=MESH))
-
+    pairs = [(counts_far, counts), (v_far, v), (metric_far, metric), (curvature_far, curvature)]
+    pairs += [(line_far, line), (plane_far, plane)]
+    copies = [pltpu.make_async_copy(*pair, local_sem.at[i]) for i, pair in enumerate(pairs)]
+    for copy in copies:
+        copy.start()
+
+    copies[0].wait()
     count = counts[my_row]
-    start = jnp.int32(0)
-    for rank in range(ranks):
-        start = start + jnp.where(rank < my_row, counts[rank], 0)
-
     kind = iota((STATES, LANES), 0)
     decay_log = jnp.where(kind % 2 == 0, FIRST["log"], SECOND["log"])
     for k in range(16):
@@ -172,23 +166,29 @@
         s_weight[k] = jnp.where(k < count, weight, 0.0)
 
     pl.semaphore_wait(barrier, planes + ranks - 2)
-
-    for piece in range(len(pieces)):
-        over_planes(lambda p, piece=piece: forth(piece, my_plane, p).start())
+    over_planes(lambda p: forth(0, my_plane, p).start())
+    copies[1].wait()
 
     @pl.loop(0, length // LANES)
     def _(tile):
         at = lanes(tile * LANES)
+        totals = [jnp.zeros((STATES, LANES), jnp.float32)] * 3
+        for k in range(16):
+            weight = s_weight[k]
+            totals = [totals[c] + weight * v[c, k // 8, pl.ds(k % 8, 1), at] for c in range(3)]
         for c in range(3):
-            total = jnp.zeros((STATES, LANES), jnp.float32)
-            for k in range(16):
-                total = total + s_weight[k] * v[c, k // 8, pl.ds(k % 8, 1), at]
-            s_out[c, :, at] = total
+            s_out[c, :, at] = totals[c]
 
     over_ranks(lambda p: state_forth(my_row, p).start())
+    over_planes(lambda p: forth(1, my_plane, p).start())
     s_in[my_row] = s_out[:, :, lanes(my_row * s_cols, s_cols)]
-    for piece, (half, part) in enumerate(pieces):
-        z_in[piece, my_plane] = v[:, half, :, lanes(my_plane * z_cols + part * LANES)]
+    for half in range(2):
+        z_in[half, my_plane] = v[:, half, :, lanes(my_plane * z_cols, z_cols)]
+
+    for copy in copies[2:]:
+        copy.wait()
+    line_high[...], line_low[...] = split(line[...])
+    plane_high[...], plane_low[...] = split(plane[...])
 
     for c in range(3):
         turned = pltpu.roll(v[c].reshape(16, length), LANES // 2, 1)
@@ -201,7 +201,8 @@
 
     group = 4
 
-    def along_x(step):
+    @pl.loop(0, length // (LANES * group))
+    def _(step):
         def windows(ref):
             return jnp.concatenate(
                 [ref[:, lanes((step * group + i) * LANES, 2 * LANES)] for i in range(group)], axis=0
@@ -216,56 +217,56 @@
                 part = both[rows, LANES:] - wind * both[rows, :LANES]
                 out[c, :, :, at] = part.reshape(2, 8, LANES)
 
-    steps_x = length // (LANES * group)
-    pl.loop(0, steps_x // 2)(along_x)
-
-    def along_z(piece):
-        over_planes(lambda p: forth(piece, p, my_plane).wait_recv())
-        held = [z_in[piece, :, c].reshape(8 * planes, LANES) for c in range(3)]
-        both = product((plane_high[...], plane_low[...]), split(jnp.concatenate(held, axis=1)))
-        for c in range(3):
-            at = slice(c * LANES, (c + 1) * LANES)
-            part = both[8 * planes :, at] - held[2] * both[: 8 * planes, at]
-            z_out[piece, :, c] = part.reshape(planes, 8, LANES)
-        over_planes(lambda p: back(piece, my_plane, p).start())
-        half, part = pieces[piece]
-        z_back[:, half, :, lanes(my_plane * z_cols + part * LANES)] = z_out[piece, my_plane]
-
-    def over_y():
-        size = ranks * STATES
-        row_rank, row_kind = iota((size, size), 0) // STATES, iota((size, size), 0) % STATES
-        col_rank, col_kind = iota((size, size), 1) // STATES, iota((size, size), 1) % STATES
-        row_start = row_count = col_start = col_count = jnp.zeros((size, size), jnp.int32)
-        for rank in range(ranks):
-            held = counts[rank]
-            row_start = row_start + jnp.where(rank < row_rank, held, 0)
-            col_start = col_start + jnp.where(rank < col_rank, held, 0)
-            row_count = jnp.where(rank == row_rank, held, row_count)
-            col_count = jnp.where(rank == col_rank, held, col_count)
+    def along_z(half):
+        over_planes(lambda p: forth(half, p, my_plane).wait_recv())
+        for part in range(z_cols // LANES):
+            cut = slice(part * LANES, (part + 1) * LANES)
+            held = [z_in[half, :, c, :, cut].reshape(8 * planes, LANES) for c in range(3)]
+            both = product((plane_high[...], plane_low[...]), split(jnp.concatenate(held, axis=1)))
+            for c in range(3):
+                at = slice(c * LANES, (c + 1) * LANES)
+                term = both[8 * planes :, at] - held[2] * both[: 8 * planes, at]
+                z_out[half, :, c, :, cut] = term.reshape(planes, 8, LANES)
+        over_planes(lambda p: back(half, my_plane, p).start())
+        z_back[:, half, :, lanes(my_plane * z_cols, z_cols)] = z_out[half, my_plane]
+
+    size = ranks * STATES
+    col_rank, col_kind = iota((8, size), 1) // STATES, iota((8, size), 1) % STATES
+    row_kind = iota((8, size), 0)
+    row_log = jnp.where(row_kind % 2 == 0, FIRST["log"], SECOND["log"])
+    col_start = col_count = jnp.zeros((8, size), jnp.int32)
+    start = jnp.int32(0)
+    for rank in range(ranks):
+        col_start = col_start + jnp.where(rank < col_rank, counts[rank], 0)
+        col_count = jnp.where(rank == col_rank, counts[rank], col_count)
+        start = start + jnp.where(rank < my_row, counts[rank], 0)
+
+    def rank_rows(rank, row_start):
+        row_count = counts[rank]
         ahead = row_start - col_start - col_count
         ahead = jnp.where(ahead < 0, ahead + live_total, ahead)
         behind = col_start - row_start - row_count
         behind = jnp.where(behind < 0, behind + live_total, behind)
-        log = jnp.where(row_kind % 2 == 0, FIRST["log"], SECOND["log"])
-        same = power(log, jnp.where(row_kind < 2, ahead, behind))
-        matrix = jnp.where((row_kind == col_kind) & (row_kind < 4), same, 0.0)
-        matrix = jnp.where((row_kind == 4) & (col_kind == 5) & (ahead == 0), 1.0, matrix)
-        matrix = jnp.where((row_kind == 5) & (col_kind == 4) & (behind == 0), 1.0, matrix)
-        matrix = split(matrix)
+        same = power(row_log, jnp.where(row_kind < 2, ahead, behind))
+        rows = jnp.where((row_kind == col_kind) & (row_kind < 4), same, 0.0)
+        rows = jnp.where((row_kind == 4) & (col_kind == 5) & (ahead == 0), 1.0, rows)
+        rows = jnp.where((row_kind == 5) & (col_kind == 4) & (behind == 0), 1.0, rows)
+        matrix[pl.ds(pl.multiple_of(rank * STATES, STATES), STATES), :] = rows
+        return row_start + row_count
+
+    lax.fori_loop(0, ranks, rank_rows, jnp.int32(0))
+
+    def over_y():
         over_ranks(lambda p: state_forth(p, my_row).wait_recv())
         held = [s_in[:, c].reshape(size, s_cols) for c in range(3)]
-        both = product(matrix, split(jnp.concatenate(held, axis=1)))
+        both = product(split(matrix[...]), split(jnp.concatenate(held, axis=1)))
         for c in range(3):
             s_mid[:, c] = both[:, c * s_cols : (c + 1) * s_cols].reshape(ranks, STATES, s_cols)
         over_ranks(lambda p: state_back(my_row, p).start())
         s_back[:, :, lanes(my_row * s_cols, s_cols)] = s_mid[my_row]
 
     along_z(0)
-    pl.loop(steps_x // 2, steps_x)(along_x)
-    along_z(1)
     over_y()
-    for piece in range(2, len(pieces)):
-        along_z(piece)
 
     for half in range(2):
         slot = iota((8, LANES), 0) + 8 * half
@@ -307,6 +308,7 @@
                 used, viscosity * (stretch * stretch * two + bend * one), 0.0
             )
 
+    along_z(1)
     over_ranks(lambda p: state_back(p, my_row).wait_recv())
 
     @pl.loop(0, length // LANES)
@@ -316,20 +318,21 @@
         for term in range(16 + 6):
             for c in range(3):
                 if term < 16:
-                    line = v[c, term // 8, pl.ds(term % 8, 1), at]
+                    row = v[c, term // 8, pl.ds(term % 8, 1), at]
                 else:
-                    line = s_back[c, pl.ds(term - 16, 1), at]
+                    row = s_back[c, pl.ds(term - 16, 1), at]
                 for half in range(2):
-                    sums[c][half] = [sums[c][half][i] + y_weight[term, half, i] * line for i in range(2)]
+                    sums[c][half] = [sums[c][half][i] + y_weight[term, half, i] * row for i in range(2)]
         for half in range(2):
             wind = v[1, half, :, at]
             for c in range(3):
                 out[c, half, :, at] += sums[c][half][1] - wind * sums[c][half][0]
 
-    per_half = len(pieces) // 2
+    def leave(half):
+        return pltpu.make_async_copy(out.at[:, half], out_far.at[:, half], local_sem.at[6 + half])
+
     for half in range(2):
-        for piece in range(half * per_half, (half + 1) * per_half):
-            over_planes(lambda p, piece=piece: back(piece, p, my_plane).wait_recv())
+        over_planes(lambda p, half=half: back(half, p, my_plane).wait_recv())
         live = iota((8, LANES), 0) + 8 * half < count
 
         @pl.loop(0, length // LANES)
@@ -338,33 +341,48 @@
             for c in range(3):
                 out[c, half, :, at] = jnp.where(live, out[c, half, :, at] + z_back[c, half, :, at], 0.0)
 
-    for piece in range(len(pieces)):
-        over_planes(lambda p, piece=piece: forth(piece, my_plane, p).wait_send())
-        over_planes(lambda p, piece=piece: back(piece, my_plane, p).wait_send())
+        leave(half).start()
+
+    for half in range(2):
+        over_planes(lambda p, half=half: forth(half, my_plane, p).wait_send())
+        over_planes(lambda p, half=half: back(half, my_plane, p).wait_send())
     over_ranks(lambda p: state_forth(my_row, p).wait_send())
     over_ranks(lambda p: state_back(my_row, p).wait_send())
+    for half in range(2):
+        leave(half).wait()
 
 
 def local(ranks, planes, velocity, row_counts, y_metric, y_curvature):
     length = velocity.shape[3]
     live_total = y_metric.shape[0]
     z_cols, s_cols = length // planes, length // ranks
-    pieces = 2 * z_cols // LANES
-    vmem = pl.BlockSpec(memory_space=pltpu.VMEM)
-    smem = pl.BlockSpec(memory_space=pltpu.SMEM)
+    far = pl.BlockSpec(memory_space=pltpu.HBM)
     whole = (3, 2, 8, length)
+    line, plane = line_table().astype(np.float32), plane_table(planes).astype(np.float32)
     dma = pltpu.SemaphoreType.DMA
-    f32 = jnp.float32
+    f32, bf16 = jnp.float32, jnp.bfloat16
     result = pl.pallas_call(
         functools.partial(kernel, ranks, planes, live_total, length),
         out_shape=jax.ShapeDtypeStruct(whole, f32),
-        in_specs=[vmem, smem, smem, smem, vmem, vmem, vmem, vmem],
-        out_specs=vmem,
+        in_specs=[far] * 6,
+        out_specs=far,
         scratch_shapes=[
-            pltpu.VMEM((48, length + LANES), jnp.bfloat16),
-            pltpu.VMEM((48, length + LANES), jnp.bfloat16),
-            pltpu.VMEM((pieces, planes, 3, 8, LANES), f32),
-            pltpu.VMEM((pieces, planes, 3, 8, LANES), f32),
+            pltpu.VMEM(whole, f32),
+            pltpu.VMEM(whole, f32),
+            pltpu.SMEM(row_counts.shape, jnp.int32),
+            pltpu.SMEM(y_metric.shape, f32),
+            pltpu.SMEM(y_curvature.shape, f32),
+            pltpu.VMEM(line.shape, f32),
+            pltpu.VMEM(plane.shape, f32),
+            pltpu.VMEM(line.shape, bf16),
+            pltpu.VMEM(line.shape, bf16),
+            pltpu.VMEM(plane.shape, bf16),
+            pltpu.VMEM(plane.shape, bf16),
+            pltpu.VMEM((ranks * STATES, ranks * STATES), f32),
+            pltpu.VMEM((48, length + LANES), bf16),
+            pltpu.VMEM((48, length + LANES), bf16),
+            pltpu.VMEM((2, planes, 3, 8, z_cols), f32),
+            pltpu.VMEM((2, planes, 3, 8, z_cols), f32),
             pltpu.VMEM(whole, f32),
             pltpu.VMEM((3, STATES, length), f32),
             pltpu.VMEM((ranks, 3, STATES, s_cols), f32),
@@ -372,23 +390,21 @@
             pltpu.VMEM((3, STATES, length), f32),
             pltpu.VMEM((16, STATES, LANES), f32),
             pltpu.VMEM((22, 2, 2, 8, LANES), f32),
-            dma((pieces, planes)),
-            dma((pieces, planes)),
-            dma((pieces, planes)),
-            dma((pieces, planes)),
+            dma((8,)),
+            dma((2, planes)),
+            dma((2, planes)),
+            dma((2, planes)),
+            dma((2, planes)),
             dma((ranks,)),
             dma((ranks,)),
             dma((ranks,)),
             dma((ranks,)),
         ],
         compiler_params=pltpu.CompilerParams(
-            collective_id=0, has_side_effects=True, vmem_limit_bytes=32 * 1024 * 1024
+            collective_id=0, has_side_effects=True, vmem_limit_bytes=63 * 1024 * 1024
         ),
         cost_estimate=pl.CostEstimate(flops=10**9, bytes_accessed=2 * 10**6, transcendentals=10**5),
-    )(
-        velocity.reshape(whole), row_counts, y_metric, y_curvature,
-        *split_table(line_table()), *split_table(plane_table(planes)),
-    )
+    )(velocity.reshape(whole), row_counts, y_metric, y_curvature, jnp.asarray(line), jnp.asarray(plane))
     return result.reshape(velocity.shape)
 
 

time: 70.1 us -> 61.6 us (0.88)
  local copies, waits for them, and re-layouts: 7.52 us -> 2.06 us
  Pallas kernels: 62.3 us -> 59.4 us
    unnamed x17 -> x1, local copies, waits for them, and re-layouts: 7.52 us -> 2.06 us
    pallas_call x1, Pallas kernels: 62.3 us -> 59.4 us  [local(): pl.pallas_call(functools.partial(kernel, ranks, planes, live_total, lengt...]
where the time goes in v1:
time: 61.6 us; the launch traced here: 61.5 us
  Pallas kernels  59.4 us (96%)
  local copies, waits for them, and re-layouts  2.06 us (3%)
    pallas_call x1, Pallas kernels, local(): pl.pallas_call(functools.partial(kernel, ranks, planes, live_total, lengt...  59.4 us
    unnamed x1, local copies, waits for them, and re-layouts  2.06 us

profile of v1, /device:TPU:1, one launch (start us, length us, event | category | flops | bytes accessed | tf_op | source)
XLA Modules:
  0.0 61.5 jit_solution(8328484781644088753)
XLA Ops:
  0.0 59.4 %shard_map.64 = f32[3,2,8,4096]{3,2,1,0:T(8,128)} custom-call(f32[3,2,8,4096]{3,2,1,0:T(8,128)} %bitcast.5, s32[32]{0:T(128)} %counts_far.1, f32[257]{0:T(512)} %metric_far.1, f32[257]{0:T(512)} %curvature_far.1, f32[256,256]{1,0:T(8,128)} %constant.4.clone.line_far, f32[256,128]{1,0:T(8,128)} %constant.5.clone.plane_far), custom_call_target="tpu_custom_call" | custom-call | flops 1000000000 | bytes 2000000 | tf_op jit(solution)/shard_map/pallas_call | solution.py:364
  59.4 2.1 %copy.9 = f32[3,1,16,4096]{3,2,1,0:T(8,128)} copy(f32[3,1,16,4096]{3,2,1,0:T(8,128)} %bitcast.4) | data formatting | bytes 1572864

commit v2 on v1

--- a/solution.py
+++ b/solution.py
@@ -90,8 +90,8 @@
     v_far, counts_far, metric_far, curvature_far, line_far, plane_far,
     out_far,
     out, v, counts, metric, curvature, line, plane, line_high, line_low, plane_high, plane_low, matrix,
-    pad_high, pad_low, z_in, z_out, z_back, s_out, s_in, s_mid, s_back, s_weight, y_weight,
-    local_sem, z_send, z_recv, zb_send, zb_recv, s_send, s_recv, sb_send, sb_recv,
+    pad_high, pad_low, z_in, z_out, z_back, relay, s_out, s_in, s_mid, s_back, s_weight, y_weight,
+    local_sem, z_send, z_recv, zb_send, zb_recv, s_send, s_recv, sb_send, sb_recv, relay_sem,
 ):
     my_row, my_plane = lax.axis_index("row"), lax.axis_index("span")
     z_cols, s_cols = length // planes, length // ranks
@@ -141,6 +141,76 @@
 
     def over_planes(act):
         pl.loop(0, planes - 1)(lambda index: act(partner(index, my_plane, planes)))
+
+    chips = planes // 2
+    reach = chips // 2
+    near = 4 * (reach - 1) + 1
+    my_chip, my_core = my_plane // 2, my_plane % 2
+
+    def over_near(act):
+        @pl.loop(0, near)
+        def _(index):
+            away = reach - 1 - index // 4
+            chip = jnp.where(index % 2 == 0, my_chip + away, my_chip + chips - away) % chips
+            act(chip * 2 + jnp.where(index == near - 1, 1 - my_core, index // 2 % 2))
+
+    def flip(place):
+        return place + 1 - 2 * (place % 2)
+
+    ahead_plane, behind_plane = (my_plane + reach) % planes, (my_plane + planes - reach) % planes
+    relays = [ahead_plane, behind_plane]
+    opposite = (my_plane + chips) % planes
+    finals = [opposite, flip(opposite)]
+    origins, goals = [behind_plane, ahead_plane], [ahead_plane, flip(behind_plane)]
+
+    def relay_copy(held, leg, half, way, src, dst, target):
+        sems = relay_sem.at[held, leg, half, way], relay_sem.at[held, 1, half, way]
+        return pltpu.make_async_remote_copy(
+            src, dst, sems[0], sems[1], device_id={"span": target}, device_id_type=MESH
+        )
+
+    def forth_first(half, way):
+        src = v_far.at[:, half, :, lanes(finals[way] * z_cols, z_cols)]
+        return relay_copy(0, 0, half, way, src, relay.at[0, half, way], relays[way])
+
+    def back_first(half, way):
+        return relay_copy(1, 0, half, way, z_out.at[half, finals[way]], relay.at[1, half, way], relays[way])
+
+    def forth_second(half, way):
+        return pltpu.make_async_remote_copy(
+            src_ref=relay.at[0, half, way],
+            dst_ref=z_in.at[half, origins[way]],
+            send_sem=relay_sem.at[0, 2, half, way],
+            recv_sem=z_recv.at[half, origins[way]],
+            device_id={"span": goals[way]},
+            device_id_type=MESH,
+        )
+
+    def back_second(half, way):
+        return pltpu.make_async_remote_copy(
+            src_ref=relay.at[1, half, way],
+            dst_ref=z_back.at[:, half, :, lanes(origins[way] * z_cols, z_cols)],
+            send_sem=relay_sem.at[1, 2, half, way],
+            recv_sem=zb_recv.at[half, origins[way]],
+            device_id={"span": goals[way]},
+            device_id_type=MESH,
+        )
+
+    def send(first, direct, half):
+        for way in range(2):
+            first(half, way).start()
+        over_near(lambda p: direct(half, my_plane, p).start())
+
+    def pass_on(first, second, half):
+        for way in range(2):
+            first(half, way).wait_recv()
+            second(half, way).start()
+
+    def sent(first, second, direct, half):
+        for way in range(2):
+            first(half, way).wait_send()
+            second(half, way).wait_send()
+        over_near(lambda p: direct(half, my_plane, p).wait_send())
 
     def over_ranks(act):
         pl.loop(0, ranks - 1)(lambda index: act(partner(index, my_row, ranks)))
@@ -166,7 +236,7 @@
         s_weight[k] = jnp.where(k < count, weight, 0.0)
 
     pl.semaphore_wait(barrier, planes + ranks - 2)
-    over_planes(lambda p: forth(0, my_plane, p).start())
+    send(forth_first, forth, 0)
     copies[1].wait()
 
     @pl.loop(0, length // LANES)
@@ -180,11 +250,12 @@
             s_out[c, :, at] = totals[c]
 
     over_ranks(lambda p: state_forth(my_row, p).start())
-    over_planes(lambda p: forth(1, my_plane, p).start())
+    send(forth_first, forth, 1)
     s_in[my_row] = s_out[:, :, lanes(my_row * s_cols, s_cols)]
     for half in range(2):
         z_in[half, my_plane] = v[:, half, :, lanes(my_plane * z_cols, z_cols)]
 
+    pass_on(forth_first, forth_second, 0)
     for copy in copies[2:]:
         copy.wait()
     line_high[...], line_low[...] = split(line[...])
@@ -227,7 +298,7 @@
                 at = slice(c * LANES, (c + 1) * LANES)
                 term = both[8 * planes :, at] - held[2] * both[: 8 * planes, at]
                 z_out[half, :, c, :, cut] = term.reshape(planes, 8, LANES)
-        over_planes(lambda p: back(half, my_plane, p).start())
+        send(back_first, back, half)
         z_back[:, half, :, lanes(my_plane * z_cols, z_cols)] = z_out[half, my_plane]
 
     size = ranks * STATES
@@ -265,8 +336,10 @@
         over_ranks(lambda p: state_back(my_row, p).start())
         s_back[:, :, lanes(my_row * s_cols, s_cols)] = s_mid[my_row]
 
+    pass_on(forth_first, forth_second, 1)
     along_z(0)
     over_y()
+    pass_on(back_first, back_second, 0)
 
     for half in range(2):
         slot = iota((8, LANES), 0) + 8 * half
@@ -311,8 +384,7 @@
     along_z(1)
     over_ranks(lambda p: state_back(p, my_row).wait_recv())
 
-    @pl.loop(0, length // LANES)
-    def _(tile):
+    def along_y(tile):
         at = lanes(tile * LANES)
         sums = [[[jnp.zeros((8, LANES), jnp.float32)] * 2 for _ in range(2)] for _ in range(3)]
         for term in range(16 + 6):
@@ -328,6 +400,16 @@
             for c in range(3):
                 out[c, half, :, at] += sums[c][half][1] - wind * sums[c][half][0]
 
+    tiles = length // LANES
+    pl.loop(0, tiles // 2)(along_y)
+    pass_on(back_first, back_second, 1)
+    pl.loop(tiles // 2, tiles)(along_y)
+    for half in range(2):
+        sent(forth_first, forth_second, forth, half)
+    over_ranks(lambda p: state_forth(my_row, p).wait_send())
+    over_ranks(lambda p: state_back(my_row, p).wait_send())
+    sent(back_first, back_second, back, 0)
+
     def leave(half):
         return pltpu.make_async_copy(out.at[:, half], out_far.at[:, half], local_sem.at[6 + half])
 
@@ -343,11 +425,7 @@
 
         leave(half).start()
 
-    for half in range(2):
-        over_planes(lambda p, half=half: forth(half, my_plane, p).wait_send())
-        over_planes(lambda p, half=half: back(half, my_plane, p).wait_send())
-    over_ranks(lambda p: state_forth(my_row, p).wait_send())
-    over_ranks(lambda p: state_back(my_row, p).wait_send())
+    sent(back_first, back_second, back, 1)
     for half in range(2):
         leave(half).wait()
 
@@ -384,6 +462,7 @@
             pltpu.VMEM((2, planes, 3, 8, z_cols), f32),
             pltpu.VMEM((2, planes, 3, 8, z_cols), f32),
             pltpu.VMEM(whole, f32),
+            pltpu.VMEM((2, 2, 2, 3, 8, z_cols), f32),
             pltpu.VMEM((3, STATES, length), f32),
             pltpu.VMEM((ranks, 3, STATES, s_cols), f32),
             pltpu.VMEM((ranks, 3, STATES, s_cols), f32),
@@ -399,6 +478,7 @@
             dma((ranks,)),
             dma((ranks,)),
             dma((ranks,)),
+            dma((2, 3, 2, 2)),
         ],
         compiler_params=pltpu.CompilerParams(
             collective_id=0, has_side_effects=True, vmem_limit_bytes=63 * 1024 * 1024

time: 61.6 us -> 60.3 us (0.979)
  Pallas kernels: 59.4 us -> 58 us
    pallas_call x1, Pallas kernels: 59.4 us -> 58 us  [local(): pl.pallas_call(functools.partial(kernel, ranks, planes, live_total, lengt...]
where the time goes in v2:
time: 60.3 us; the launch traced here: 60.1 us
  Pallas kernels  58 us (96%)
  local copies, waits for them, and re-layouts  2.06 us (3%)
    pallas_call x1, Pallas kernels, local(): pl.pallas_call(functools.partial(kernel, ranks, planes, live_total, lengt...  58 us
    unnamed x1, local copies, waits for them, and re-layouts  2.06 us

profile of v2, /device:TPU:1, one launch (start us, length us, event | category | flops | bytes accessed | tf_op | source)
XLA Modules:
  0.0 60.1 jit_solution(7393855766432057756)
XLA Ops:
  0.0 58.0 %shard_map.64 = f32[3,2,8,4096]{3,2,1,0:T(8,128)} custom-call(f32[3,2,8,4096]{3,2,1,0:T(8,128)} %bitcast.5, s32[32]{0:T(128)} %counts_far.1, f32[257]{0:T(512)} %metric_far.1, f32[257]{0:T(512)} %curvature_far.1, f32[256,256]{1,0:T(8,128)} %constant.4.clone.line_far, f32[256,128]{1,0:T(8,128)} %constant.5.clone.plane_far), custom_call_target="tpu_custom_call" | custom-call | flops 1000000000 | bytes 2000000 | tf_op jit(solution)/shard_map/pallas_call | solution.py:442
  58.0 2.1 %copy.9 = f32[3,1,16,4096]{3,2,1,0:T(8,128)} copy(f32[3,1,16,4096]{3,2,1,0:T(8,128)} %bitcast.4) | data formatting | bytes 1572864

commit v3 on v1

--- a/solution.py
+++ b/solution.py
@@ -88,9 +88,9 @@
 def kernel(
     ranks, planes, live_total, length,
     v_far, counts_far, metric_far, curvature_far, line_far, plane_far,
-    out_far,
+    out_far, z_back,
     out, v, counts, metric, curvature, line, plane, line_high, line_low, plane_high, plane_low, matrix,
-    pad_high, pad_low, z_in, z_out, z_back, s_out, s_in, s_mid, s_back, s_weight, y_weight,
+    pad_high, pad_low, z_in, z_out, s_out, s_in, s_mid, s_back, s_weight, y_weight,
     local_sem, z_send, z_recv, zb_send, zb_recv, s_send, s_recv, sb_send, sb_recv,
 ):
     my_row, my_plane = lax.axis_index("row"), lax.axis_index("span")
@@ -166,10 +166,11 @@
         s_weight[k] = jnp.where(k < count, weight, 0.0)
 
     pl.semaphore_wait(barrier, planes + ranks - 2)
-    over_planes(lambda p: forth(0, my_plane, p).start())
+    for half in range(2):
+        over_planes(lambda p, half=half: forth(half, my_plane, p).start())
     copies[1].wait()
 
-    @pl.loop(0, length // LANES)
+    @pl.loop(0, length // LANES, unroll=2)
     def _(tile):
         at = lanes(tile * LANES)
         totals = [jnp.zeros((STATES, LANES), jnp.float32)] * 3
@@ -180,7 +181,6 @@
             s_out[c, :, at] = totals[c]
 
     over_ranks(lambda p: state_forth(my_row, p).start())
-    over_planes(lambda p: forth(1, my_plane, p).start())
     s_in[my_row] = s_out[:, :, lanes(my_row * s_cols, s_cols)]
     for half in range(2):
         z_in[half, my_plane] = v[:, half, :, lanes(my_plane * z_cols, z_cols)]
@@ -199,10 +199,9 @@
         pad_high[rows, pl.ds(length, LANES)] = high[:, :LANES]
         pad_low[rows, pl.ds(length, LANES)] = low[:, :LANES]
 
-    group = 4
-
-    @pl.loop(0, length // (LANES * group))
-    def _(step):
+    group = 8
+
+    def along_x(step):
         def windows(ref):
             return jnp.concatenate(
                 [ref[:, lanes((step * group + i) * LANES, 2 * LANES)] for i in range(group)], axis=0
@@ -217,8 +216,13 @@
                 part = both[rows, LANES:] - wind * both[rows, :LANES]
                 out[c, :, :, at] = part.reshape(2, 8, LANES)
 
+    def keep(half):
+        own = z_back.at[:, half, :, lanes(my_plane * z_cols, z_cols)]
+        return pltpu.make_async_copy(z_out.at[half, my_plane], own, local_sem.at[7 + half])
+
     def along_z(half):
         over_planes(lambda p: forth(half, p, my_plane).wait_recv())
+        live = iota((planes, 8, LANES), 1) + 8 * half < count
         for part in range(z_cols // LANES):
             cut = slice(part * LANES, (part + 1) * LANES)
             held = [z_in[half, :, c, :, cut].reshape(8 * planes, LANES) for c in range(3)]
@@ -226,9 +230,11 @@
             for c in range(3):
                 at = slice(c * LANES, (c + 1) * LANES)
                 term = both[8 * planes :, at] - held[2] * both[: 8 * planes, at]
-                z_out[half, :, c, :, cut] = term.reshape(planes, 8, LANES)
+                z_out[half, :, c, :, cut] = jnp.where(live, term.reshape(planes, 8, LANES), 0.0)
         over_planes(lambda p: back(half, my_plane, p).start())
-        z_back[:, half, :, lanes(my_plane * z_cols, z_cols)] = z_out[half, my_plane]
+        keep(half).start()
+
+    pl.loop(0, length // (LANES * group))(along_x)
 
     size = ranks * STATES
     col_rank, col_kind = iota((8, size), 1) // STATES, iota((8, size), 1) % STATES
@@ -254,7 +260,7 @@
         matrix[pl.ds(pl.multiple_of(rank * STATES, STATES), STATES), :] = rows
         return row_start + row_count
 
-    lax.fori_loop(0, ranks, rank_rows, jnp.int32(0))
+    lax.fori_loop(0, ranks, rank_rows, jnp.int32(0), unroll=4)
 
     def over_y():
         over_ranks(lambda p: state_forth(p, my_row).wait_recv())
@@ -264,9 +270,6 @@
             s_mid[:, c] = both[:, c * s_cols : (c + 1) * s_cols].reshape(ranks, STATES, s_cols)
         over_ranks(lambda p: state_back(my_row, p).start())
         s_back[:, :, lanes(my_row * s_cols, s_cols)] = s_mid[my_row]
-
-    along_z(0)
-    over_y()
 
     for half in range(2):
         slot = iota((8, LANES), 0) + 8 * half
@@ -308,11 +311,15 @@
                 used, viscosity * (stretch * stretch * two + bend * one), 0.0
             )
 
+    along_z(0)
     along_z(1)
+    over_y()
+    for half in range(2):
+        over_planes(lambda p, half=half: forth(half, my_plane, p).wait_send())
+    over_ranks(lambda p: state_forth(my_row, p).wait_send())
     over_ranks(lambda p: state_back(p, my_row).wait_recv())
 
-    @pl.loop(0, length // LANES)
-    def _(tile):
+    def along_y(tile):
         at = lanes(tile * LANES)
         sums = [[[jnp.zeros((8, LANES), jnp.float32)] * 2 for _ in range(2)] for _ in range(3)]
         for term in range(16 + 6):
@@ -325,31 +332,40 @@
                     sums[c][half] = [sums[c][half][i] + y_weight[term, half, i] * row for i in range(2)]
         for half in range(2):
             wind = v[1, half, :, at]
+            live = iota((8, LANES), 0) + 8 * half < count
             for c in range(3):
-                out[c, half, :, at] += sums[c][half][1] - wind * sums[c][half][0]
-
-    def leave(half):
-        return pltpu.make_async_copy(out.at[:, half], out_far.at[:, half], local_sem.at[6 + half])
-
+                term = out[c, half, :, at] + sums[c][half][1] - wind * sums[c][half][0]
+                out[c, half, :, at] = jnp.where(live, term, 0.0)
+
+    pl.loop(0, length // LANES)(along_y)
+    leave = pltpu.make_async_copy(out, out_far, local_sem.at[6])
+    leave.start()
+    over_ranks(lambda p: state_back(my_row, p).wait_send())
+    for half in range(2):
+        over_planes(lambda p, half=half: back(half, my_plane, p).wait_send())
     for half in range(2):
         over_planes(lambda p, half=half: back(half, p, my_plane).wait_recv())
-        live = iota((8, LANES), 0) + 8 * half < count
-
-        @pl.loop(0, length // LANES)
-        def _(tile, half=half, live=live):
-            at = lanes(tile * LANES)
-            for c in range(3):
-                out[c, half, :, at] = jnp.where(live, out[c, half, :, at] + z_back[c, half, :, at], 0.0)
-
-        leave(half).start()
-
-    for half in range(2):
-        over_planes(lambda p, half=half: forth(half, my_plane, p).wait_send())
-        over_planes(lambda p, half=half: back(half, my_plane, p).wait_send())
-    over_ranks(lambda p: state_forth(my_row, p).wait_send())
-    over_ranks(lambda p: state_back(my_row, p).wait_send())
-    for half in range(2):
-        leave(half).wait()
+        keep(half).wait()
+    leave.wait()
+
+
+def add_kernel(left_far, right_far, out_far, left, right, load_sem, store_sem):
+    def load(c, i):
+        return pltpu.make_async_copy((left_far, right_far)[i].at[c], (left, right)[i].at[c], load_sem.at[c, i])
+
+    def store(c):
+        return pltpu.make_async_copy(left.at[c], out_far.at[c], store_sem.at[c])
+
+    for c in range(3):
+        for i in range(2):
+            load(c, i).start()
+    for c in range(3):
+        for i in range(2):
+            load(c, i).wait()
+        left[c] = left[c] + right[c]
+        store(c).start()
+    for c in range(3):
+        store(c).wait()
 
 
 def local(ranks, planes, velocity, row_counts, y_metric, y_curvature):
@@ -361,11 +377,11 @@
     line, plane = line_table().astype(np.float32), plane_table(planes).astype(np.float32)
     dma = pltpu.SemaphoreType.DMA
     f32, bf16 = jnp.float32, jnp.bfloat16
-    result = pl.pallas_call(
+    parts = pl.pallas_call(
         functools.partial(kernel, ranks, planes, live_total, length),
-        out_shape=jax.ShapeDtypeStruct(whole, f32),
+        out_shape=[jax.ShapeDtypeStruct(whole, f32)] * 2,
         in_specs=[far] * 6,
-        out_specs=far,
+        out_specs=[far] * 2,
         scratch_shapes=[
             pltpu.VMEM(whole, f32),
             pltpu.VMEM(whole, f32),
@@ -383,14 +399,13 @@
             pltpu.VMEM((48, length + LANES), bf16),
             pltpu.VMEM((2, planes, 3, 8, z_cols), f32),
             pltpu.VMEM((2, planes, 3, 8, z_cols), f32),
-            pltpu.VMEM(whole, f32),
             pltpu.VMEM((3, STATES, length), f32),
             pltpu.VMEM((ranks, 3, STATES, s_cols), f32),
             pltpu.VMEM((ranks, 3, STATES, s_cols), f32),
             pltpu.VMEM((3, STATES, length), f32),
             pltpu.VMEM((16, STATES, LANES), f32),
             pltpu.VMEM((22, 2, 2, 8, LANES), f32),
-            dma((8,)),
+            dma((9,)),
             dma((2, planes)),
             dma((2, planes)),
             dma((2, planes)),
@@ -405,6 +420,15 @@
         ),
         cost_estimate=pl.CostEstimate(flops=10**9, bytes_accessed=2 * 10**6, transcendentals=10**5),
     )(velocity.reshape(whole), row_counts, y_metric, y_curvature, jnp.asarray(line), jnp.asarray(plane))
+    result = pl.pallas_call(
+        add_kernel,
+        out_shape=jax.ShapeDtypeStruct(whole, f32),
+        in_specs=[far] * 2,
+        out_specs=far,
+        scratch_shapes=[pltpu.VMEM(whole, f32), pltpu.VMEM(whole, f32), dma((3, 2)), dma((3,))],
+        compiler_params=pltpu.CompilerParams(vmem_limit_bytes=63 * 1024 * 1024),
+        cost_estimate=pl.CostEstimate(flops=2 * 10**5, bytes_accessed=2 * 10**6, transcendentals=0),
+    )(*parts)
     return result.reshape(velocity.shape)
 
 

time: 61.6 us -> 59.5 us (0.966)
  local copies, waits for them, and re-layouts: 2.06 us -> 0 us
    pallas_call x1, Pallas kernels: 59.4 us -> 57.2 us  [local(): pl.pallas_call(functools.partial(kernel, ranks, planes, live_total, lengt...]
    pallas_call x0 -> x1, Pallas kernels: none -> 2.15 us  [local(): pl.pallas_call(add_kernel, out_shape=jax.ShapeDtypeStruct(whole, f32), in...]
    unnamed x1 -> x0, local copies, waits for them, and re-layouts: 2.06 us -> none
where the time goes in v3:
time: 59.5 us; the launch traced here: 59.4 us
  Pallas kernels  59.4 us (100%)
    pallas_call x1, Pallas kernels, local(): pl.pallas_call(functools.partial(kernel, ranks, planes, live_total, lengt...  57.2 us
    pallas_call x1, Pallas kernels, local(): pl.pallas_call(add_kernel, out_shape=jax.ShapeDtypeStruct(whole, f32), in...  2.15 us

profile of v3, /device:TPU:1, one launch (start us, length us, event | category | flops | bytes accessed | tf_op | source)
XLA Modules:
  0.0 59.4 jit_solution(4406481788180765012)
XLA Ops:
  0.0 57.2 %shard_map.64 = (f32[3,2,8,4096]{3,2,1,0:T(8,128)}, f32[3,2,8,4096]{3,2,1,0:T(8,128)}) custom-call(f32[3,2,8,4096]{3,2,1,0:T(8,128)} %bitcast.4, s32[32]{0:T(128)} %counts_far.1, f32[257]{0:T(512)} %metric_far.1, f32[257]{0:T(512)} %curvature_far.1, f32[256,256]{1,0:T(8,128)} %constant.4.clone.line_far, f32[256,128]{1,0:T(8,128)} %constant.5.clone.plane_far), custom_call_target="tpu_custom_call" | custom-call | flops 1000000000 | bytes 2000000 | tf_op jit(solution)/shard_map/pallas_call | solution.py:380
  57.2 2.2 %shard_map.65 = f32[3,2,8,4096]{3,2,1,0:T(8,128)} custom-call(f32[3,2,8,4096]{3,2,1,0:T(8,128)} %get-tuple-element.7.left_far, f32[3,2,8,4096]{3,2,1,0:T(8,128)} %get-tuple-element.8.right_far), custom_call_target="tpu_custom_call" | custom-call | flops 200000 | bytes 2000000 | tf_op jit(solution)/shard_map/pallas_call | solution.py:423

commit v4 on v3

--- a/solution.py
+++ b/solution.py
@@ -72,17 +72,26 @@
 
 def power(log, steps):
     size = jnp.exp(steps.astype(jnp.float32) * log)
-    return jnp.where(steps % 2 == 0, size, -size)
+    return jnp.where((steps & 1) == 0, size, -size)
 
 
 def iota(shape, axis):
     return lax.broadcasted_iota(jnp.int32, shape, axis)
 
 
-def partner(index, me, count):
+def over(count, me, act):
     half = count // 2
-    step = jnp.where(index % 2 == 1, half - (index + 1) // 2, half + index // 2)
-    return (me + step) % count
+
+    def at(step):
+        other = me + step
+        act(jnp.where(other >= count, other - count, other), step)
+
+    at(half)
+
+    @pl.loop(0, half - 1)
+    def _(index):
+        at(half - 1 - index)
+        at(half + 1 + index)
 
 
 def kernel(
@@ -99,55 +108,55 @@
     def lanes(start, size=LANES):
         return pl.ds(pl.multiple_of(start, LANES), size)
 
-    def forth(half, source, target):
+    def forth(half, source, target, step):
         return pltpu.make_async_remote_copy(
             src_ref=v_far.at[:, half, :, lanes(target * z_cols, z_cols)],
             dst_ref=z_in.at[half, source],
-            send_sem=z_send.at[half, target],
-            recv_sem=z_recv.at[half, source],
-            device_id={"span": target},
+            send_sem=z_send.at[half, step],
+            recv_sem=z_recv.at[half, step],
+            device_id=(my_row, target),
             device_id_type=MESH,
         )
 
-    def back(half, source, target):
+    def back(half, source, target, step):
         return pltpu.make_async_remote_copy(
             src_ref=z_out.at[half, target],
             dst_ref=z_back.at[:, half, :, lanes(source * z_cols, z_cols)],
-            send_sem=zb_send.at[half, target],
-            recv_sem=zb_recv.at[half, source],
-            device_id={"span": target},
+            send_sem=zb_send.at[half, step],
+            recv_sem=zb_recv.at[half, step],
+            device_id=(my_row, target),
             device_id_type=MESH,
         )
 
-    def state_forth(source, target):
+    def state_forth(source, target, step):
         return pltpu.make_async_remote_copy(
             src_ref=s_out.at[:, :, lanes(target * s_cols, s_cols)],
             dst_ref=s_in.at[source],
-            send_sem=s_send.at[target],
-            recv_sem=s_recv.at[source],
-            device_id={"row": target},
+            send_sem=s_send.at[step],
+            recv_sem=s_recv.at[step],
+            device_id=(target, my_plane),
             device_id_type=MESH,
         )
 
-    def state_back(source, target):
+    def state_back(source, target, step):
         return pltpu.make_async_remote_copy(
             src_ref=s_mid.at[target],
             dst_ref=s_back.at[:, :, lanes(source * s_cols, s_cols)],
-            send_sem=sb_send.at[target],
-            recv_sem=sb_recv.at[source],
-            device_id={"row": target},
+            send_sem=sb_send.at[step],
+            recv_sem=sb_recv.at[step],
+            device_id=(target, my_plane),
             device_id_type=MESH,
         )
 
     def over_planes(act):
-        pl.loop(0, planes - 1)(lambda index: act(partner(index, my_plane, planes)))
+        over(planes, my_plane, act)
 
     def over_ranks(act):
-        pl.loop(0, ranks - 1)(lambda index: act(partner(index, my_row, ranks)))
+        over(ranks, my_row, act)
 
     barrier = pltpu.get_barrier_semaphore()
-    over_planes(lambda p: pl.semaphore_signal(barrier, 1, device_id={"span": p}, device_id_type=MESH))
-    over_ranks(lambda p: pl.semaphore_signal(barrier, 1, device_id={"row": p}, device_id_type=MESH))
+    over_planes(lambda p, _: pl.semaphore_signal(barrier, 1, device_id=(my_row, p), device_id_type=MESH))
+    over_ranks(lambda p, _: pl.semaphore_signal(barrier, 1, device_id=(p, my_plane), device_id_type=MESH))
     pairs = [(counts_far, counts), (v_far, v), (metric_far, metric), (curvature_far, curvature)]
     pairs += [(line_far, line), (plane_far, plane)]
     copies = [pltpu.make_async_copy(*pair, local_sem.at[i]) for i, pair in enumerate(pairs)]
@@ -167,7 +176,7 @@
 
     pl.semaphore_wait(barrier, planes + ranks - 2)
     for half in range(2):
-        over_planes(lambda p, half=half: forth(half, my_plane, p).start())
+        over_planes(lambda p, step, half=half: forth(half, my_plane, p, step).start())
     copies[1].wait()
 
     @pl.loop(0, length // LANES, unroll=2)
@@ -180,7 +189,7 @@
         for c in range(3):
             s_out[c, :, at] = totals[c]
 
-    over_ranks(lambda p: state_forth(my_row, p).start())
+    over_ranks(lambda p, step: state_forth(my_row, p, step).start())
     s_in[my_row] = s_out[:, :, lanes(my_row * s_cols, s_cols)]
     for half in range(2):
         z_in[half, my_plane] = v[:, half, :, lanes(my_plane * z_cols, z_cols)]
@@ -221,7 +230,7 @@
         return pltpu.make_async_copy(z_out.at[half, my_plane], own, local_sem.at[7 + half])
 
     def along_z(half):
-        over_planes(lambda p: forth(half, p, my_plane).wait_recv())
+        over_planes(lambda p, step: forth(half, p, my_plane, planes - step).wait_recv())
         live = iota((planes, 8, LANES), 1) + 8 * half < count
         for part in range(z_cols // LANES):
             cut = slice(part * LANES, (part + 1) * LANES)
@@ -231,7 +240,7 @@
                 at = slice(c * LANES, (c + 1) * LANES)
                 term = both[8 * planes :, at] - held[2] * both[: 8 * planes, at]
                 z_out[half, :, c, :, cut] = jnp.where(live, term.reshape(planes, 8, LANES), 0.0)
-        over_planes(lambda p: back(half, my_plane, p).start())
+        over_planes(lambda p, step: back(half, my_plane, p, step).start())
         keep(half).start()
 
     pl.loop(0, length // (LANES * group))(along_x)
@@ -263,12 +272,12 @@
     lax.fori_loop(0, ranks, rank_rows, jnp.int32(0), unroll=4)
 
     def over_y():
-        over_ranks(lambda p: state_forth(p, my_row).wait_recv())
+        over_ranks(lambda p, step: state_forth(p, my_row, ranks - step).wait_recv())
         held = [s_in[:, c].reshape(size, s_cols) for c in range(3)]
         both = product(split(matrix[...]), split(jnp.concatenate(held, axis=1)))
         for c in range(3):
             s_mid[:, c] = both[:, c * s_cols : (c + 1) * s_cols].reshape(ranks, STATES, s_cols)
-        over_ranks(lambda p: state_back(my_row, p).start())
+        over_ranks(lambda p, step: state_back(my_row, p, step).start())
         s_back[:, :, lanes(my_row * s_cols, s_cols)] = s_mid[my_row]
 
     for half in range(2):
@@ -315,9 +324,9 @@
     along_z(1)
     over_y()
     for half in range(2):
-        over_planes(lambda p, half=half: forth(half, my_plane, p).wait_send())
-    over_ranks(lambda p: state_forth(my_row, p).wait_send())
-    over_ranks(lambda p: state_back(p, my_row).wait_recv())
+        over_planes(lambda p, step, half=half: forth(half, my_plane, p, step).wait_send())
+    over_ranks(lambda p, step: state_forth(my_row, p, step).wait_send())
+    over_ranks(lambda p, step: state_back(p, my_row, ranks - step).wait_recv())
 
     def along_y(tile):
         at = lanes(tile * LANES)
@@ -340,11 +349,11 @@
     pl.loop(0, length // LANES)(along_y)
     leave = pltpu.make_async_copy(out, out_far, local_sem.at[6])
     leave.start()
-    over_ranks(lambda p: state_back(my_row, p).wait_send())
-    for half in range(2):
-        over_planes(lambda p, half=half: back(half, my_plane, p).wait_send())
-    for half in range(2):
-        over_planes(lambda p, half=half: back(half, p, my_plane).wait_recv())
+    over_ranks(lambda p, step: state_back(my_row, p, step).wait_send())
+    for half in range(2):
+        over_planes(lambda p, step, half=half: back(half, my_plane, p, step).wait_send())
+    for half in range(2):
+        over_planes(lambda p, step, half=half: back(half, p, my_plane, planes - step).wait_recv())
         keep(half).wait()
     leave.wait()
 

time: 59.5 us -> 58.1 us (0.976)
  Pallas kernels: 59.4 us -> 57.9 us
    pallas_call x1, Pallas kernels: 57.2 us -> 55.8 us  [local(): pl.pallas_call(functools.partial(kernel, ranks, planes, live_total, lengt...]
where the time goes in v4:
time: 58.1 us; the launch traced here: 57.9 us
  Pallas kernels  57.9 us (100%)
    pallas_call x1, Pallas kernels, local(): pl.pallas_call(functools.partial(kernel, ranks, planes, live_total, lengt...  55.8 us
    pallas_call x1, Pallas kernels, local(): pl.pallas_call(add_kernel, out_shape=jax.ShapeDtypeStruct(whole, f32), in...  2.15 us

profile of v4, /device:TPU:1, one launch (start us, length us, event | category | flops | bytes accessed | tf_op | source)
XLA Modules:
  0.0 57.9 jit_solution(8495938590175124831)
XLA Ops:
  0.0 55.8 %shard_map.64 = (f32[3,2,8,4096]{3,2,1,0:T(8,128)}, f32[3,2,8,4096]{3,2,1,0:T(8,128)}) custom-call(f32[3,2,8,4096]{3,2,1,0:T(8,128)} %bitcast.4, s32[32]{0:T(128)} %counts_far.1, f32[257]{0:T(512)} %metric_far.1, f32[257]{0:T(512)} %curvature_far.1, f32[256,256]{1,0:T(8,128)} %constant.4.clone.line_far, f32[256,128]{1,0:T(8,128)} %constant.5.clone.plane_far), custom_call_target="tpu_custom_call" | custom-call | flops 1000000000 | bytes 2000000 | tf_op jit(solution)/shard_map/pallas_call | solution.py:389
  55.8 2.2 %shard_map.65 = f32[3,2,8,4096]{3,2,1,0:T(8,128)} custom-call(f32[3,2,8,4096]{3,2,1,0:T(8,128)} %get-tuple-element.7.left_far, f32[3,2,8,4096]{3,2,1,0:T(8,128)} %get-tuple-element.8.right_far), custom_call_target="tpu_custom_call" | custom-call | flops 200000 | bytes 2000000 | tf_op jit(solution)/shard_map/pallas_call | solution.py:432

commit v5 on v4

--- a/solution.py
+++ b/solution.py
@@ -175,8 +175,7 @@
         s_weight[k] = jnp.where(k < count, weight, 0.0)
 
     pl.semaphore_wait(barrier, planes + ranks - 2)
-    for half in range(2):
-        over_planes(lambda p, step, half=half: forth(half, my_plane, p, step).start())
+    over_planes(lambda p, step: forth(0, my_plane, p, step).start())
     copies[1].wait()
 
     @pl.loop(0, length // LANES, unroll=2)
@@ -207,6 +206,8 @@
         pad_low[rows, pl.ds(0, length)] = low
         pad_high[rows, pl.ds(length, LANES)] = high[:, :LANES]
         pad_low[rows, pl.ds(length, LANES)] = low[:, :LANES]
+
+    over_planes(lambda p, step: forth(1, my_plane, p, step).start())
 
     group = 8
 
@@ -359,22 +360,24 @@
 
 
 def add_kernel(left_far, right_far, out_far, left, right, load_sem, store_sem):
-    def load(c, i):
-        return pltpu.make_async_copy((left_far, right_far)[i].at[c], (left, right)[i].at[c], load_sem.at[c, i])
-
-    def store(c):
-        return pltpu.make_async_copy(left.at[c], out_far.at[c], store_sem.at[c])
-
-    for c in range(3):
+    parts = [(c, half) for c in range(3) for half in range(2)]
+
+    def load(at, i):
+        return pltpu.make_async_copy((left_far, right_far)[i].at[at], (left, right)[i].at[at], load_sem.at[*at, i])
+
+    def store(at):
+        return pltpu.make_async_copy(left.at[at], out_far.at[at], store_sem.at[*at])
+
+    for at in parts:
         for i in range(2):
-            load(c, i).start()
-    for c in range(3):
+            load(at, i).start()
+    for at in parts:
         for i in range(2):
-            load(c, i).wait()
-        left[c] = left[c] + right[c]
-        store(c).start()
-    for c in range(3):
-        store(c).wait()
+            load(at, i).wait()
+        left[at] = left[at] + right[at]
+        store(at).start()
+    for at in parts:
+        store(at).wait()
 
 
 def local(ranks, planes, velocity, row_counts, y_metric, y_curvature):
@@ -434,7 +437,7 @@
         out_shape=jax.ShapeDtypeStruct(whole, f32),
         in_specs=[far] * 2,
         out_specs=far,
-        scratch_shapes=[pltpu.VMEM(whole, f32), pltpu.VMEM(whole, f32), dma((3, 2)), dma((3,))],
+        scratch_shapes=[pltpu.VMEM(whole, f32), pltpu.VMEM(whole, f32), dma((3, 2, 2)), dma((3, 2))],
         compiler_params=pltpu.CompilerParams(vmem_limit_bytes=63 * 1024 * 1024),
         cost_estimate=pl.CostEstimate(flops=2 * 10**5, bytes_accessed=2 * 10**6, transcendentals=0),
     )(*parts)

time: 58.1 us -> 58.2 us (level)
  no operation moved by 1% of the time
where the time goes in v5:
time: 58.2 us; the launch traced here: 58 us
  Pallas kernels  58 us (100%)
    pallas_call x1, Pallas kernels, local(): pl.pallas_call(functools.partial(kernel, ranks, planes, live_total, lengt...  55.8 us
    pallas_call x1, Pallas kernels, local(): pl.pallas_call(add_kernel, out_shape=jax.ShapeDtypeStruct(whole, f32), in...  2.27 us

profile of v5, /device:TPU:1, one launch (start us, length us, event | category | flops | bytes accessed | tf_op | source)
XLA Modules:
  0.0 58.0 jit_solution(17109192735343949485)
XLA Ops:
  0.0 55.8 %shard_map.64 = (f32[3,2,8,4096]{3,2,1,0:T(8,128)}, f32[3,2,8,4096]{3,2,1,0:T(8,128)}) custom-call(f32[3,2,8,4096]{3,2,1,0:T(8,128)} %bitcast.4, s32[32]{0:T(128)} %counts_far.1, f32[257]{0:T(512)} %metric_far.1, f32[257]{0:T(512)} %curvature_far.1, f32[256,256]{1,0:T(8,128)} %constant.4.clone.line_far, f32[256,128]{1,0:T(8,128)} %constant.5.clone.plane_far), custom_call_target="tpu_custom_call" | custom-call | flops 1000000000 | bytes 2000000 | tf_op jit(solution)/shard_map/pallas_call | solution.py:392
  55.8 2.3 %shard_map.65 = f32[3,2,8,4096]{3,2,1,0:T(8,128)} custom-call(f32[3,2,8,4096]{3,2,1,0:T(8,128)} %get-tuple-element.7.left_far, f32[3,2,8,4096]{3,2,1,0:T(8,128)} %get-tuple-element.8.right_far), custom_call_target="tpu_custom_call" | custom-call | flops 200000 | bytes 2000000 | tf_op jit(solution)/shard_map/pallas_call | solution.py:435

commit v6 on v4

--- a/solution.py
+++ b/solution.py
@@ -99,8 +99,8 @@
     v_far, counts_far, metric_far, curvature_far, line_far, plane_far,
     out_far, z_back,
     out, v, counts, metric, curvature, line, plane, line_high, line_low, plane_high, plane_low, matrix,
-    pad_high, pad_low, z_in, z_out, s_out, s_in, s_mid, s_back, s_weight, y_weight,
-    local_sem, z_send, z_recv, zb_send, zb_recv, s_send, s_recv, sb_send, sb_recv,
+    pad_high, pad_low, z_in, z_out, relay, s_out, s_in, s_mid, s_back, s_weight, y_weight,
+    local_sem, z_send, z_recv, zb_send, zb_recv, s_send, s_recv, sb_send, sb_recv, relay_sem,
 ):
     my_row, my_plane = lax.axis_index("row"), lax.axis_index("span")
     z_cols, s_cols = length // planes, length // ranks
@@ -153,6 +153,82 @@
 
     def over_ranks(act):
         over(ranks, my_row, act)
+
+    chips, my_core = planes // 2, my_plane % 2
+    reach = chips // 2
+    far_steps = [chips, chips + 1 - 2 * my_core]
+
+    def around(step):
+        place = my_plane + step
+        return jnp.where(place >= planes, place - planes, place)
+
+    relays = [around(reach), around(planes - reach)]
+    finals = [around(step) for step in far_steps]
+    origins = [around(planes - reach), around(reach)]
+    goals = [around(reach), around(planes - reach) + 1 - 2 * my_core]
+
+    def over_near(act):
+        def at(step):
+            act(around(step), step)
+
+        at(chips - 1 + 2 * my_core)
+
+        @pl.loop(1, chips - 1)
+        def _(index):
+            at(chips - 1 - index)
+            at(chips + 1 + index)
+
+    def relay_first(held, half, way, src):
+        return pltpu.make_async_remote_copy(
+            src_ref=src,
+            dst_ref=relay.at[held, half, way],
+            send_sem=relay_sem.at[held, 0, half, way],
+            recv_sem=relay_sem.at[held, 1, half, way],
+            device_id=(my_row, relays[way]),
+            device_id_type=MESH,
+        )
+
+    def forth_first(half, way):
+        return relay_first(0, half, way, v_far.at[:, half, :, lanes(finals[way] * z_cols, z_cols)])
+
+    def back_first(half, way):
+        return relay_first(1, half, way, z_out.at[half, finals[way]])
+
+    def forth_second(half, way):
+        return pltpu.make_async_remote_copy(
+            src_ref=relay.at[0, half, way],
+            dst_ref=z_in.at[half, origins[way]],
+            send_sem=relay_sem.at[0, 2, half, way],
+            recv_sem=z_recv.at[half, far_steps[way]],
+            device_id=(my_row, goals[way]),
+            device_id_type=MESH,
+        )
+
+    def back_second(half, way):
+        return pltpu.make_async_remote_copy(
+            src_ref=relay.at[1, half, way],
+            dst_ref=z_back.at[:, half, :, lanes(origins[way] * z_cols, z_cols)],
+            send_sem=relay_sem.at[1, 2, half, way],
+            recv_sem=zb_recv.at[half, far_steps[way]],
+            device_id=(my_row, goals[way]),
+            device_id_type=MESH,
+        )
+
+    def send(first, direct, half):
+        for way in range(2):
+            first(half, way).start()
+        over_near(lambda p, step: direct(half, my_plane, p, step).start())
+
+    def pass_on(first, second, half):
+        for way in range(2):
+            first(half, way).wait_recv()
+            second(half, way).start()
+
+    def sent(first, second, direct, half):
+        for way in range(2):
+            first(half, way).wait_send()
+            second(half, way).wait_send()
+        over_near(lambda p, step: direct(half, my_plane, p, step).wait_send())
 
     barrier = pltpu.get_barrier_semaphore()
     over_planes(lambda p, _: pl.semaphore_signal(barrier, 1, device_id=(my_row, p), device_id_type=MESH))
@@ -175,8 +251,7 @@
         s_weight[k] = jnp.where(k < count, weight, 0.0)
 
     pl.semaphore_wait(barrier, planes + ranks - 2)
-    for half in range(2):
-        over_planes(lambda p, step, half=half: forth(half, my_plane, p, step).start())
+    send(forth_first, forth, 0)
     copies[1].wait()
 
     @pl.loop(0, length // LANES, unroll=2)
@@ -207,6 +282,9 @@
         pad_low[rows, pl.ds(0, length)] = low
         pad_high[rows, pl.ds(length, LANES)] = high[:, :LANES]
         pad_low[rows, pl.ds(length, LANES)] = low[:, :LANES]
+
+    send(forth_first, forth, 1)
+    pass_on(forth_first, forth_second, 0)
 
     group = 8
 
@@ -240,10 +318,11 @@
                 at = slice(c * LANES, (c + 1) * LANES)
                 term = both[8 * planes :, at] - held[2] * both[: 8 * planes, at]
                 z_out[half, :, c, :, cut] = jnp.where(live, term.reshape(planes, 8, LANES), 0.0)
-        over_planes(lambda p, step: back(half, my_plane, p, step).start())
+        send(back_first, back, half)
         keep(half).start()
 
     pl.loop(0, length // (LANES * group))(along_x)
+    pass_on(forth_first, forth_second, 1)
 
     size = ranks * STATES
     col_rank, col_kind = iota((8, size), 1) // STATES, iota((8, size), 1) % STATES
@@ -322,9 +401,11 @@
 
     along_z(0)
     along_z(1)
+    pass_on(back_first, back_second, 0)
     over_y()
+    pass_on(back_first, back_second, 1)
     for half in range(2):
-        over_planes(lambda p, step, half=half: forth(half, my_plane, p, step).wait_send())
+        sent(forth_first, forth_second, forth, half)
     over_ranks(lambda p, step: state_forth(my_row, p, step).wait_send())
     over_ranks(lambda p, step: state_back(p, my_row, ranks - step).wait_recv())
 
@@ -351,7 +432,7 @@
     leave.start()
     over_ranks(lambda p, step: state_back(my_row, p, step).wait_send())
     for half in range(2):
-        over_planes(lambda p, step, half=half: back(half, my_plane, p, step).wait_send())
+        sent(back_first, back_second, back, half)
     for half in range(2):
         over_planes(lambda p, step, half=half: back(half, p, my_plane, planes - step).wait_recv())
         keep(half).wait()
@@ -408,6 +489,7 @@
             pltpu.VMEM((48, length + LANES), bf16),
             pltpu.VMEM((2, planes, 3, 8, z_cols), f32),
             pltpu.VMEM((2, planes, 3, 8, z_cols), f32),
+            pltpu.VMEM((2, 2, 2, 3, 8, z_cols), f32),
             pltpu.VMEM((3, STATES, length), f32),
             pltpu.VMEM((ranks, 3, STATES, s_cols), f32),
             pltpu.VMEM((ranks, 3, STATES, s_cols), f32),
@@ -423,6 +505,7 @@
             dma((ranks,)),
             dma((ranks,)),
             dma((ranks,)),
+            dma((2, 3, 2, 2)),
         ],
         compiler_params=pltpu.CompilerParams(
             collective_id=0, has_side_effects=True, vmem_limit_bytes=63 * 1024 * 1024

time: 58.1 us -> 60 us (1.033)
  Pallas kernels: 57.9 us -> 59.9 us
    pallas_call x1, Pallas kernels: 55.8 us -> 57.7 us  [local(): pl.pallas_call(functools.partial(kernel, ranks, planes, live_total, lengt...]
where the time goes in v6:
time: 60 us; the launch traced here: 59.9 us
  Pallas kernels  59.9 us (100%)
    pallas_call x1, Pallas kernels, local(): pl.pallas_call(functools.partial(kernel, ranks, planes, live_total, lengt...  57.7 us
    pallas_call x1, Pallas kernels, local(): pl.pallas_call(add_kernel, out_shape=jax.ShapeDtypeStruct(whole, f32), in...  2.15 us

profile of v6, /device:TPU:1, one launch (start us, length us, event | category | flops | bytes accessed | tf_op | source)
XLA Modules:
  0.0 59.9 jit_solution(10385511864101045624)
XLA Ops:
  0.0 57.7 %shard_map.64 = (f32[3,2,8,4096]{3,2,1,0:T(8,128)}, f32[3,2,8,4096]{3,2,1,0:T(8,128)}) custom-call(f32[3,2,8,4096]{3,2,1,0:T(8,128)} %bitcast.4, s32[32]{0:T(128)} %counts_far.1, f32[257]{0:T(512)} %metric_far.1, f32[257]{0:T(512)} %curvature_far.1, f32[256,256]{1,0:T(8,128)} %constant.4.clone.line_far, f32[256,128]{1,0:T(8,128)} %constant.5.clone.plane_far), custom_call_target="tpu_custom_call" | custom-call | flops 1000000000 | bytes 2000000 | tf_op jit(solution)/shard_map/pallas_call | solution.py:470
  57.7 2.2 %shard_map.65 = f32[3,2,8,4096]{3,2,1,0:T(8,128)} custom-call(f32[3,2,8,4096]{3,2,1,0:T(8,128)} %get-tuple-element.7.left_far, f32[3,2,8,4096]{3,2,1,0:T(8,128)} %get-tuple-element.8.right_far), custom_call_target="tpu_custom_call" | custom-call | flops 200000 | bytes 2000000 | tf_op jit(solution)/shard_map/pallas_call | solution.py:515
